TPU v7x, 32 devices: a whole 2x2x4 slice. The times are simulated.
32 devices in a mesh: groups: 2 (over y), leaf: 4 (over z), level: 2 (over x), sub: 2 (over core).
Axes of the slice: x: 2, y: 2, z: 4, core: 2. Of those that a mesh axis runs over, the one named last changes fastest.
Arguments:
- rhs: float32 [64, 262144], P(('level', 'sub'), ('groups', 'leaf')), parts along dimension 1, may hold values from -6 to 6
- points: float32 [3, 262144], P(None, ('groups', 'leaf')), parts along dimension 1, may hold values from 0 to 2
- basis: float32 [32, 262144], P(None, ('groups', 'leaf')), parts along dimension 1, may hold values from -0.75 to 0.75
- transfer: float32 [32, 261632], P(None, ('groups', 'leaf')), parts along dimension 1, may hold values from -0.875 to 0.875
- leaf_proxies: float32 [3, 131072], P(None, ('groups', 'leaf')), parts along dimension 1, may hold values from 0 to 2
- root_proxies: float32 [3, 256], P(None, 'groups'), parts along dimension 1, may hold values from 0 to 2
- near_src: int32 [4096, 8], P(('groups', 'leaf')), parts along dimension 0, may hold values from 0 to 2047, as said below
- near_count: int32 [4096], P(('groups', 'leaf')), parts along dimension 0, may hold values from 1 to 8, as said below
- far_src: int32 [4096, 16], P(('groups', 'leaf')), parts along dimension 0, may hold values from 0 to 2047, as said below
Outputs:
- product: float32 [64, 262144], P(('level', 'sub'), ('groups', 'leaf')), parts along dimension 1
There are 2 independent parts, one for each index of `groups`. A program takes and returns all parts, laid end to end along the dimension named above; each array names one. Nothing has to cross between parts.
Inputs may be any that keep to these rules, and one draw needn't show every extreme that they name: `near_src`: each entry of row t lies within 512 of t; in every draw some row names t + 512 and some row t - 512; entries may repeat. Entries 0 to near_count[t] - 1 of row t of near_src are live, the rest are ignored; some leaf has 8. `far_src`: each entry of row t lies within 512 of t; in every draw some row names t + 512 and some row t - 512; entries may repeat.
All inputs are finite; a program needn't handle non-finite values.
Results may differ from a plain program's by a relative error of at most 0.00017.
Values sent between devices are 32-bit elements; how exact they have to be, the bound alone decides.
No kernel may reach another device: no remote copies, remote signals or barrier semaphores. Data moves between devices by JAX's collectives and lax.ppermute only.
A program may use at most 192 MiB of HBM per device.

v0:
```python
import functools
import math

import jax
import jax.numpy as jnp
import numpy as np
from jax import lax
from jax.experimental import pallas as pl
from jax.experimental.pallas import tpu as pltpu
from jax.sharding import PartitionSpec as P

spread_sq = 0.5
LANES = 128
FEATS = 16
UNROLL = 64
WIDE = 2
STEPS = 8
VMEM_LIMIT = 58 * 1024 * 1024
f32, bf16, i32 = jnp.float32, jnp.bfloat16, jnp.int32

NN = (((1,), (0,)), ((), ()))
NT = (((1,), (1,)), ((), ()))


def dot(a, b, dims=NN):
    return lax.dot_general(a, b, dims, preferred_element_type=f32)


def halves(x):
    hi = x.astype(bf16).astype(f32)
    return hi, x - hi


def stacked(x):
    hi, lo = halves(x)
    return jnp.concatenate([hi, lo], axis=0).astype(bf16)


def two_term(x, terms, dims):
    rows = x.shape[0]
    xs = stacked(x)
    high = dot(xs, terms[0], dims)
    low = dot(xs, terms[1], dims)
    return (high[:rows] + high[rows:]) + (low[:rows] + low[rows:])


def in_chunks(count, most, run):
    size = min(count, most)
    if count == size:
        run(0, size)
    else:

        def step(i, carry):
            run(i * size, size)
            return carry

        lax.fori_loop(0, count // size, step, 0)


def at(i, size):
    first = i * size
    return pl.ds(first if isinstance(first, int) else pl.multiple_of(first, size), size)


def span_of(first, n):
    start = first * LANES
    return pl.ds(start if isinstance(start, int) else pl.multiple_of(start, LANES), n * LANES)


def group_mask(shape, row_width, col_width):
    row = lax.broadcasted_iota(i32, shape, 0) // row_width
    col = lax.broadcasted_iota(i32, shape, 1) // col_width
    return row == col


def spread_rows(mat, copies, mask):
    zero = jnp.zeros((), bf16)
    parts = [part.astype(bf16) for part in halves(mat)]
    return [jnp.where(mask, jnp.concatenate([part] * copies, axis=0), zero) for part in parts]


def whole(n):
    return [pl.BlockSpec(memory_space=pltpu.VMEM)] * n


def call_blocks(body, out_shape, widths, rows, steps, nbytes):
    block = lambda r, w: pl.BlockSpec((r, w // steps), lambda i: (0, i))
    return pl.pallas_call(
        body,
        out_shape=out_shape,
        grid=(steps,),
        in_specs=[block(r, w) for r, w in zip(rows, widths)],
        out_specs=block(*out_shape.shape),
        compiler_params=pltpu.CompilerParams(vmem_limit_bytes=VMEM_LIMIT),
        cost_estimate=pl.CostEstimate(flops=0, bytes_accessed=nbytes, transcendentals=0),
    )


def call(body, out_shape, n_in, scratch=(), nbytes=0, prefetch=False):
    specs = ([pl.BlockSpec(memory_space=pltpu.SMEM)] if prefetch else []) + whole(n_in)
    return pl.pallas_call(
        body,
        out_shape=out_shape,
        in_specs=specs,
        out_specs=pl.BlockSpec(memory_space=pltpu.VMEM),
        scratch_shapes=list(scratch),
        compiler_params=pltpu.CompilerParams(vmem_limit_bytes=VMEM_LIMIT),
        cost_estimate=pl.CostEstimate(flops=0, bytes_accessed=nbytes, transcendentals=0),
    )


def leaf_coefs(rhs, basis, leaf_pts):
    rows, width = rhs.shape
    rank = basis.shape[0]
    per = LANES // rank
    span = per * leaf_pts

    def body(x_ref, b_ref, o_ref):
        mask = group_mask((per * rank, span), rank, leaf_pts)

        def run(first, n):
            ids = [first + j for j in range(n)]
            ins = [(x_ref[:, at(i, span)], b_ref[:, at(i, span)]) for i in ids]
            outs = [two_term(x, spread_rows(m, per, mask), NT) for x, m in ins]
            for i, out in zip(ids, outs):
                o_ref[:, at(i, LANES)] = out

        in_chunks(width // span // STEPS, 8, run)

    out = jax.ShapeDtypeStruct((rows, width // leaf_pts * rank), f32)
    return call_blocks(body, out, (width, width), (rows, rank), STEPS, 4 * 10**7)(rhs, basis)


def leaf_product(down, couple, basis, near, leaf_pts):
    rows, width = near.shape
    rank = basis.shape[0]
    per = LANES // rank
    span = per * leaf_pts

    def body(d_ref, c_ref, b_ref, n_ref, o_ref):
        mask = group_mask((per * rank, span), rank, leaf_pts)

        def run(first, n):
            ids = [first + j for j in range(n)]
            ins = [
                (d_ref[:, at(i, LANES)] + c_ref[:, at(i, LANES)], b_ref[:, at(i, span)]) for i in ids
            ]
            outs = [two_term(x, spread_rows(m, per, mask), NN) for x, m in ins]
            for i, out in zip(ids, outs):
                o_ref[:, at(i, span)] = n_ref[:, at(i, span)] + out

        in_chunks(width // span // STEPS, 8, run)

    out = jax.ShapeDtypeStruct((rows, width), f32)
    far = down.shape[1]
    sizes = (far, far, width, width), (rows, rows, rank, rows)
    return call_blocks(body, out, *sizes, STEPS, 4 * 10**7)(down, couple, basis, near)


def tree_up(coef, transfer, leaves):
    rows, width = coef.shape
    rank = transfer.shape[0]
    levels = leaves.bit_length() - 1

    def body(c_ref, e_ref, o_ref, buf):
        for level in range(levels):
            here = leaves >> level
            offset = (2 * leaves - 2 * here) * rank
            share = 1 if level == 0 else 2
            out_span = min(LANES, here * rank)
            groups = out_span // rank * share
            span = groups * rank
            mask = group_mask((span, out_span), share * rank, rank)
            src = c_ref if level == 0 else buf.at[(level - 1) % 2]
            dst = buf.at[level % 2]

            def run(first, n):
                ids = [first + j for j in range(n)]
                base = offset // out_span
                ins = [(src[:, at(i, span)], e_ref[:, at(base + i, out_span)]) for i in ids]
                outs = [two_term(x, spread_rows(m, groups, mask), NN) for x, m in ins]
                for i, out in zip(ids, outs):
                    dst[:, at(i, out_span)] = out

            in_chunks(here * rank // out_span, 8, run)
        last = buf[(levels - 1) % 2, :, : 2 * rank]
        o_ref[...] = last[:, :rank] + last[:, rank:]

    return call(
        body,
        jax.ShapeDtypeStruct((rows, rank), f32),
        2,
        [pltpu.VMEM((2, rows, width), f32)],
        nbytes=4 * 10**7,
    )(coef, transfer)


def tree_down(root, transfer, leaves):
    rows = root.shape[0]
    rank = transfer.shape[0]
    levels = leaves.bit_length() - 1
    width = leaves * rank

    def body(r_ref, e_ref, o_ref, buf):
        top = r_ref[...]
        buf[levels % 2, :, : 2 * rank] = jnp.concatenate([top, top], axis=1)
        for level in reversed(range(levels)):
            here = leaves >> level
            offset = (2 * leaves - 2 * here) * rank
            share = 1 if level == 0 else 2
            in_span = min(LANES, here * rank)
            groups = in_span // rank * share
            span = groups * rank
            mask = group_mask((span, in_span), share * rank, rank)
            src = buf.at[(level + 1) % 2]
            dst = o_ref if level == 0 else buf.at[level % 2]

            def run(first, n):
                ids = [first + j for j in range(n)]
                base = offset // in_span
                ins = [(src[:, at(i, in_span)], e_ref[:, at(base + i, in_span)]) for i in ids]
                outs = [two_term(x, spread_rows(m, groups, mask), NT) for x, m in ins]
                for i, out in zip(ids, outs):
                    dst[:, at(i, span)] = out

            in_chunks(here * rank // in_span, 8, run)

    return call(
        body,
        jax.ShapeDtypeStruct((rows, width), f32),
        2,
        [pltpu.VMEM((2, rows, width), f32)],
        nbytes=4 * 10**7,
    )(root, transfer)


LOG2E = math.log2(math.e)


def selections():
    source, target = np.zeros((FEATS, FEATS), np.float32), np.zeros((FEATS, FEATS), np.float32)
    for d in range(3):
        for row, (p, q) in enumerate(((0, 0), (0, 1), (1, 0), (1, 1))):
            target[3 * row + d, 8 * p + d] = 1.0
            source[3 * row + d, 8 * q + d] = 1.0
    for row, term in ((12, 3), (13, 11)):
        source[row, term] = 1.0
        target[row, 4] = 1.0
        target[row + 2, term] = 1.0
        source[row + 2, 4] = 1.0
    return source, target


def features(coords, selection, scale):
    c = jnp.concatenate([coords - 1.0, jnp.zeros((5, coords.shape[1]), f32)], axis=0)
    row = lax.broadcasted_iota(i32, c.shape, 0)
    square = (-LOG2E / spread_sq) * jnp.sum(c * c, axis=0, keepdims=True)
    terms = jnp.where(row == 3, square, jnp.where(row == 4, 1.0, c * scale))
    return dot(selection, stacked(terms))


def work_list(idx, live, group, dummy):
    count, listed = idx.shape
    items = count * (listed // group)
    livei = live.astype(i32)
    rank = jnp.sum(
        livei[:, None, :] * (jnp.arange(listed)[None, None, :] < jnp.arange(listed)[None, :, None]),
        axis=2,
    )
    slot = jnp.arange(listed, dtype=i32)
    hit = live[:, :, None] & (rank[:, :, None] == slot[None, None, :])
    total = jnp.sum(livei, axis=1)
    packed = jnp.sum(jnp.where(hit, idx[:, :, None], 0), axis=1)
    packed = jnp.where(slot[None, :] < total[:, None], packed, dummy)
    need = (total + group - 1) // group
    upto = jnp.arange(count)
    start = jnp.sum(jnp.where(upto[None, :] < upto[:, None], need[None, :], 0), axis=1)
    end = start + need
    k = jnp.arange(items, dtype=i32)
    one_hot = (start[None, :] <= k[:, None]) & (k[:, None] < end[None, :])
    target = jnp.sum(jnp.where(one_hot, upto[None, :].astype(i32), 0), axis=1)
    within = jnp.sum(jnp.where(one_hot, k[:, None] - start[None, :], 0), axis=1)
    rows = jnp.einsum(
        "kt,tm->km", one_hot.astype(f32), packed.astype(f32), precision=lax.Precision.HIGHEST
    )
    rows = jnp.round(rows).astype(i32).reshape(items, listed // group, group)
    pick = within[:, None, None] == jnp.arange(listed // group)[None, :, None]
    sources = jnp.sum(jnp.where(pick, rows, 0), axis=1)
    used = jnp.sum(need)
    sources = jnp.where((k < used)[:, None], sources, dummy)
    steps = (used + UNROLL - 1) // UNROLL
    return jnp.concatenate([target, sources.T.reshape(-1), steps[None]]), items


def pair_sums(listing, items, coords, offset, sources, leaves, pts):
    rows = sources[0].shape[0]
    width = leaves * pts
    per = LANES // pts
    pieces = len(sources)
    held = pieces * leaves
    group = WIDE * per
    narrow = per > 2
    pick_source, pick_target = selections()
    eye = np.eye(LANES, dtype=np.float32)
    consts = [jnp.asarray(m, bf16) for m in (pick_source, pick_target, eye)]

    def body(list_ref, pick_s_ref, pick_t_ref, eye_ref, *refs):
        coord_refs = refs[:pieces]
        x_refs = refs[pieces : 2 * pieces]
        o_ref, tab, targets_tab, acc = refs[2 * pieces : 2 * pieces + 4]
        flat = refs[-1]
        lane = lax.broadcasted_iota(i32, (1, LANES), 1) // pts

        def fill_targets(first, n):
            here = span_of(first + offset // LANES, n)
            feats = features(coord_refs[pieces // 2][:, here], pick_t_ref[...], 2.0 * LOG2E / spread_sq).astype(bf16)
            outs = [
                dot(eye_ref[...], feats[:, j * LANES : (j + 1) * LANES], NT).astype(bf16)
                for j in range(n)
            ]
            for j, out in enumerate(outs):
                for g in range(per):
                    targets_tab[(first + j) * per + g] = out[g * pts : (g + 1) * pts]

        in_chunks(width // LANES, 32, fill_targets)

        def repeated(rec):
            turned = [rec] + [pltpu.roll(rec, pts * j, 1) for j in range(1, per)]
            outs = []
            for j in range(per):
                out = turned[(per - j) % per]
                for g in range(1, per):
                    out = jnp.where(lane == g, turned[(g - j) % per], out)
                outs.append(out.astype(bf16))
            return outs

        def fill_narrow(piece, first, n, feats):
            outs, upright = [], []
            for c in range(n):
                outs += repeated(feats[:, c * LANES : (c + 1) * LANES])
                x = stacked(x_refs[piece][:, at(first + c, LANES)])
                upright.append(dot(eye_ref[...], x, NT).astype(bf16))
            for j, out in enumerate(outs):
                tab[piece * leaves + first * per + j] = out
            for c, out in enumerate(upright):
                for j in range(per):
                    flat[piece * leaves + (first + c) * per + j] = out[j * pts : (j + 1) * pts]

        for piece in range(pieces):

            def fill(first, n):
                feats = features(
                    coord_refs[piece][:, span_of(first + offset // LANES, n)], pick_s_ref[...], 1.0
                )
                if narrow:
                    fill_narrow(piece, first, n, feats)
                    return
                hi, lo = halves(x_refs[piece][:, span_of(first, n)])
                whole_rec = jnp.concatenate([feats, hi, lo], axis=0)
                outs = []
                for c in range(n):
                    outs += repeated(whole_rec[:, c * LANES : (c + 1) * LANES])
                for j, out in enumerate(outs):
                    tab[piece * leaves + first * per + j] = out

            in_chunks(width // LANES, 16, fill)
        tab[held] = jnp.zeros(tab.shape[1:], bf16)
        if narrow:
            flat[held] = jnp.zeros(flat.shape[1:], bf16)

        def clear(first, n):
            for j in range(n):
                acc[first + j] = jnp.zeros(acc.shape[1:], f32)

        in_chunks(leaves, 32, clear)

        masks = [
            lax.broadcasted_iota(i32, (tab.shape[1], LANES), 1) >= g * pts
            for g in range(1, per)
        ]

        def step(n, carry):
            ks = [n * UNROLL + u for u in range(UNROLL)]
            targets = [list_ref[k] for k in ks]
            recs, values = [], []
            for k in ks:
                picks = [list_ref[(g + 1) * items + k] for g in range(group)]
                blocks = []
                for w in range(WIDE):
                    rec = tab[picks[w * per]]
                    for g in range(1, per):
                        rec = jnp.where(masks[g - 1], tab[picks[w * per + g]], rec)
                    blocks.append(rec)
                recs.append(jnp.concatenate(blocks, axis=1))
                if narrow:
                    values.append(jnp.concatenate([flat[pick] for pick in picks], axis=0))
                else:
                    values.append(recs[-1][FEATS:])
            logs = [dot(targets_tab[t], rec[:FEATS]) for t, rec in zip(targets, recs)]
            kernels = [jnp.exp2(e) for e in logs]
            his = [k.astype(bf16) for k in kernels]
            los = [(k - h.astype(f32)).astype(bf16) for k, h in zip(kernels, his)]
            outs = []
            for value, hi, lo in zip(values, his, los):
                both = jnp.concatenate([hi, lo], axis=0)
                if narrow:
                    out = dot(both, value, NN)
                    outs.append(out[:pts] + out[pts:])
                else:
                    out = dot(value, both, NT)
                    outs.append(out[:rows] + out[rows:])
            for t, out in zip(targets, outs):
                acc[t] += out
            return carry

        lax.fori_loop(0, list_ref[(group + 1) * items], step, 0)

        def lay(start, n):
            outs = []
            for c in range(n):
                first = (start + c) * per
                if narrow:
                    out = jnp.concatenate([acc[first + j] for j in range(per)], axis=0).T
                    outs.append(out[:rows] + out[rows:])
                else:
                    for j in range(per):
                        one = acc[first + j]
                        one = one + pltpu.roll(one, pts, 1)
                        out = one if j == 0 else jnp.where(lane == j, one, out)
                    outs.append(out)
            for c, out in enumerate(outs):
                o_ref[:, at(start + c, LANES)] = out

        in_chunks(width // LANES, 16, lay)

    scratch = [
        pltpu.VMEM((held + 1, FEATS + (0 if narrow else 2 * rows), LANES), bf16),
        pltpu.VMEM((leaves, pts, FEATS), bf16),
        pltpu.VMEM((leaves, pts, 2 * rows) if narrow else (leaves, rows, LANES), f32),
    ]
    if narrow:
        scratch.append(pltpu.VMEM((held + 1, pts, 2 * rows), bf16))
    args = [listing, *consts, *coords, *sources]
    return call(
        body,
        jax.ShapeDtypeStruct((rows, width), f32),
        len(args) - 1,
        scratch,
        nbytes=15 * 10**7,
        prefetch=True,
    )(*args)


def local(rhs, points, basis, transfer, leaf_proxies, root_proxies, near_src, near_count, far_src):
    highest = lax.Precision.HIGHEST
    rows, width = rhs.shape
    leaves = near_src.shape[0]
    leaf_pts = width // leaves
    rank = basis.shape[0]
    near_max = near_src.shape[1]
    owner = lax.axis_index("leaf")
    size = lax.axis_size("leaf")
    up = [(i, (i + 1) % size) for i in range(size - 1)]
    down_pairs = [(j, i) for i, j in up]
    both_ways = lambda x: (lax.ppermute(x, "leaf", up), lax.ppermute(x, "leaf", down_pairs))

    coords = jnp.concatenate([points, leaf_proxies], axis=1)
    halo_coords = both_ways(coords)
    coef = leaf_coefs(rhs, basis, leaf_pts)

    anchor = (owner - 1) * leaves
    live = jnp.arange(near_max, dtype=i32)[None, :] < near_count[:, None]
    near_list = work_list(near_src - anchor, live, WIDE * LANES // leaf_pts, 3 * leaves)
    far_live = jnp.ones(far_src.shape, bool)
    far_list = work_list(far_src - anchor, far_live, WIDE * LANES // rank, 3 * leaves)

    root = tree_up(coef, transfer, leaves)
    halo_coords, coef, root = lax.optimization_barrier((halo_coords, coef, root))
    coords = [halo_coords[0], coords, halo_coords[1]]
    halo_coef = both_ways(coef)
    parts, origins = [], []
    for s in range(2, size):
        rise, fall = [(i, i + s) for i in range(size - s)], [(i + s, i) for i in range(size - s)]
        if 2 * s >= size:
            parts.append(lax.ppermute(root, "leaf", rise + fall))
            origins.append(jnp.where(owner >= s, owner - s, owner + s))
        else:
            parts += [lax.ppermute(root, "leaf", rise), lax.ppermute(root, "leaf", fall)]
            origins += [owner - s, owner + s]

    own_proxy = lax.dynamic_slice_in_dim(root_proxies, owner * rank, rank, 1)
    top = jnp.zeros((rows, rank), f32)
    for part, origin in zip(parts, origins):
        there = (origin >= 0) & (origin < size)
        start = jnp.clip(origin, 0, size - 1) * rank
        proxy = lax.dynamic_slice_in_dim(root_proxies, start, rank, 1)
        dist = jnp.sum((own_proxy[:, :, None] - proxy[:, None, :]) ** 2, axis=0)
        kernel = jnp.where(there, jnp.exp(-dist / spread_sq), 0.0)
        top = top + jnp.einsum("aj,rj->ra", kernel, part, precision=highest)
    down = tree_down(top, transfer, leaves)

    halo_coef, down, sent = lax.optimization_barrier((halo_coef, down, rhs))
    halo_rhs = both_ways(sent)
    couple = pair_sums(
        *far_list, coords, width, [halo_coef[0], coef, halo_coef[1]], leaves, rank
    )
    halo_rhs, couple = lax.optimization_barrier((halo_rhs, couple))
    near = pair_sums(
        *near_list, coords, 0, [halo_rhs[0], rhs, halo_rhs[1]], leaves, leaf_pts
    )
    return leaf_product(down, couple, basis, near, leaf_pts)


def solution(mesh):
    in_specs = (
        P(("level", "sub"), ("groups", "leaf")),
        P(None, ("groups", "leaf")),
        P(None, ("groups", "leaf")),
        P(None, ("groups", "leaf")),
        P(None, ("groups", "leaf")),
        P(None, "groups"),
        P(("groups", "leaf"), None),
        P(("groups", "leaf")),
        P(("groups", "leaf"), None),
    )
    out_specs = P(("level", "sub"), ("groups", "leaf"))
    return jax.shard_map(local, mesh=mesh, in_specs=in_specs, out_specs=out_specs, check_vma=False)
```

profile of v0, /device:TPU:4, one launch (start us, length us, event | category | flops | bytes accessed | tf_op | source)
XLA Modules:
  0.0 196.7 jit_solution(11781403602003517696)
XLA Ops:
  0.0 1.1 constant_dynamic-update-slice_fusion.1
  1.1 1.0 constant_dynamic-update-slice_fusion.refs_1_
  2.2 0.0 copy-start.2
  2.2 1.3 collective-permute-start.1
  3.5 4.6 %collective-permute-start = (f32[3,49152]{1,0:T(4,128)S(1)}, f32[3,49152]{1,0:T(4,128)S(1)}, u32[]{:S(2)}, u32[]{:S(2)}) collective-permute-start(f32[3,49152]{1,0:T(4,128)S(1)} %constant_dynamic-update-slice_fusion.refs_1_), channel_id=1, source_target_pairs={{0,4},{4,8},{8,12},{1,5},{5,9},{9,13},{2,6},{6,10},{10,14},{3,7},{... | collective-permute-start | bytes 1769480 | tf_op jit(solution)/shard_map/ppermute | solution.py:465
  8.1 0.7 convert_reduce_fusion.1
  8.8 0.7 iota_compare_fusion.10
  9.5 0.7 fusion.66
  10.1 0.1 select_reduce_fusion.4
  10.3 0.7 broadcast_subtract_fusion.1
  11.0 0.1 multiply_reduce_fusion
  11.2 9.9 %shard_map.145.c_ref.refs_4_ = f32[16,16384]{1,0:T(8,128)} custom-call(f32[16,32768]{1,0:T(8,128)} %refs_4_.1, f32[32,32768]{1,0:T(8,128)} %b_ref.3), custom_call_target="tpu_custom_call" | custom-call | bytes 40000000 | tf_op jit(solution)/shard_map/pallas_call | solution.py:131
  21.1 0.0 copy-done.2
  21.1 0.0 copy-start
  21.1 0.0 copy-start.6
  21.1 12.1 %shard_map.146 = f32[16,32]{1,0:T(8,128)} custom-call(f32[16,16384]{1,0:T(8,128)} %shard_map.145.c_ref.refs_4_, f32[32,32704]{1,0:T(8,128)} %e_ref.3), custom_call_target="tpu_custom_call" | custom-call | bytes 40000000 | tf_op jit(solution)/shard_map/pallas_call | solution.py:189
  33.2 1.2 fusion.24
  34.4 1.1 select_reduce_fusion.1
  35.5 0.0 collective-permute-done.1.refs_2_
  35.5 0.0 copy-start.3
  35.5 0.0 collective-permute-done.refs_0_
  35.6 0.0 copy-done
  35.6 0.0 copy-start.4
  35.6 1.3 collective-permute-start.3
  36.9 5.5 %collective-permute-start.2 = (f32[16,16384]{1,0:T(8,128)S(1)}, f32[16,16384]{1,0:T(8,128)}, u32[]{:S(2)}, u32[]{:S(2)}) collective-permute-start(f32[16,16384]{1,0:T(8,128)S(1)} %copy-done), channel_id=1, source_target_pairs={{0,4},{4,8},{8,12},{1,5},{5,9},{9,13},{2,6},{6,10},{10,14},{3,7},{... | collective-permute-start | bytes 3145736 | tf_op jit(solution)/shard_map/ppermute | solution.py:465
  42.4 0.0 copy-done.6
  42.4 0.1 constant_dynamic-slice_fusion
  42.5 0.1 multiply_reduce_fusion.2
  42.6 3.4 %collective-permute-start.5 = (f32[16,32]{1,0:T(8,128)}, f32[16,32]{1,0:T(8,128)S(1)}, u32[]{:S(2)}, u32[]{:S(2)}) collective-permute-start(f32[16,32]{1,0:T(8,128)} %shard_map.146), channel_id=1, source_target_pairs={{0,12},{12,0},{1,13},{13,1},{2,14},{14,2},{3,15},{15,3},{16,28},{2... | collective-permute-start | bytes 6152 | tf_op jit(solution)/shard_map/ppermute | solution.py:485
  46.0 0.6 iota_compare_fusion.16
  47.3 0.1 collective-permute-start.4
  47.4 16.7 %collective-permute-done.5 = f32[16,32]{1,0:T(8,128)S(1)} collective-permute-done((f32[16,32]{1,0:T(8,128)}, f32[16,32]{1,0:T(8,128)S(1)}, u32[]{:S(2)}, u32[]{:S(2)}) %collective-permute-start.5) | collective-permute-done | bytes 2080 | tf_op jit(solution)/shard_map/ppermute | solution.py:485
  64.1 0.1 fusion.38
  64.2 0.0 collective-permute-done.4
  64.3 0.0 copy-done.3
  64.3 0.0 copy-done.4
  64.3 0.8 convolution_add_fusion.r_ref
  65.0 0.0 copy-start.1
  65.0 0.0 copy-start.5
  65.0 17.1 %shard_map.147.d_ref = f32[16,16384]{1,0:T(8,128)} custom-call(f32[16,32]{1,0:T(8,128)} %convolution_add_fusion.r_ref, f32[32,32704]{1,0:T(8,128)} %e_ref.3), custom_call_target="tpu_custom_call" | custom-call | bytes 40000000 | tf_op jit(solution)/shard_map/pallas_call | solution.py:228
  82.1 0.0 collective-permute-done.3.refs_5_
  82.1 0.0 collective-permute-done.2.refs_3_
  82.1 0.0 copy-done.1
  82.1 1.3 collective-permute-start.7
  83.4 5.9 %collective-permute-start.6 = (f32[16,32768]{1,0:T(8,128)S(1)}, f32[16,32768]{1,0:T(8,128)}, u32[]{:S(2)}, u32[]{:S(2)}) collective-permute-start(f32[16,32768]{1,0:T(8,128)S(1)} %copy-done.1), channel_id=1, source_target_pairs={{0,4},{4,8},{8,12},{1,5},{5,9},{9,13},{2,6},{6,10},{10,14},{3,7},{... | collective-permute-start | bytes 6291464 | tf_op jit(solution)/shard_map/ppermute | solution.py:465
  89.3 0.1 convert_reduce_fusion
  89.5 0.2 select_reduce_fusion.5
  89.6 0.0 copy-done.5
  89.7 0.1 select_reduce_fusion.6
  89.8 1.1 select_reduce_fusion.3
  90.9 1.2 fusion.18
  92.1 0.6 pad_add_fusion.1.list_ref
  92.8 0.6 pad_add_fusion.list_ref
  93.4 43.8 %shard_map.148.c_ref = f32[16,16384]{1,0:T(8,128)} custom-call(s32[9217]{0:T(1024)} %pad_add_fusion.list_ref, bf16[16,16]{1,0:T(8,128)(2,1)} %constant.148.clone.pick_s_ref, bf16[16,16]{1,0:T(8,128)(2,1)} %constant.149.clone.pick_t_ref, bf16[128,128]{1,0:T(8,128)(2,1)} %constant.150.clone.eye_ref, f32[3,49152]{1,0:T(4,128)} %copy-done.4, ...), custom_call_target="tpu_custom_call" | custom-call | bytes 150000000 | tf_op jit(solution)/shard_map/pallas_call | solution.py:444
  137.2 0.0 collective-permute-done.7.refs_5_
  137.2 0.0 collective-permute-done.6.refs_3_
  137.2 50.6 %shard_map.149.n_ref = f32[16,32768]{1,0:T(8,128)} custom-call(s32[5121]{0:T(1024)} %pad_add_fusion.1.list_ref, bf16[16,16]{1,0:T(8,128)(2,1)} %constant.148.clone.pick_s_ref, bf16[16,16]{1,0:T(8,128)(2,1)} %constant.149.clone.pick_t_ref, bf16[128,128]{1,0:T(8,128)(2,1)} %constant.150.clone.eye_ref, f32[3,49152]{1,0:T(4,128)} %copy-done.4, ...), custom_call_target="tpu_custom_call" | custom-call | bytes 150000000 | tf_op jit(solution)/shard_map/pallas_call | solution.py:444
  187.8 8.9 %shard_map.150 = f32[16,32768]{1,0:T(8,128)} custom-call(f32[16,16384]{1,0:T(8,128)} %shard_map.147.d_ref, f32[16,16384]{1,0:T(8,128)} %shard_map.148.c_ref, f32[32,32768]{1,0:T(8,128)} %b_ref.3, f32[16,32768]{1,0:T(8,128)} %shard_map.149.n_ref), custom_call_target="tpu_custom_call" | custom-call | bytes 40000000 | tf_op jit(solution)/shard_map/pallas_call | solution.py:157
  (14 shorter events, 0.1 us)
Async XLA Ops:
  2.2 18.9 %copy-start.2 = (f32[3,49152]{1,0:T(4,128)}, f32[3,49152]{1,0:T(4,128)S(1)}, u32[]{:S(2)}) copy-start(f32[3,49152]{1,0:T(4,128)S(1)} %constant_dynamic-update-slice_fusion.refs_1_) | copy-start | bytes 1769476
  2.2 33.4 %collective-permute-start.1 = (f32[3,49152]{1,0:T(4,128)S(1)}, f32[3,49152]{1,0:T(4,128)S(1)}, u32[]{:S(2)}, u32[]{:S(2)}) collective-permute-start(f32[3,49152]{1,0:T(4,128)S(1)} %constant_dynamic-update-slice_fusion.refs_1_), channel_id=1, source_target_pairs={{4,0},{8,4},{12,8},{5,1},{9,5},{13,9},{6,2},{10,6},{14,10},{7,3},{... | collective-permute-start | bytes 1769480 | tf_op jit(solution)/shard_map/ppermute | solution.py:465
  3.5 32.1 %collective-permute-start = (f32[3,49152]{1,0:T(4,128)S(1)}, f32[3,49152]{1,0:T(4,128)S(1)}, u32[]{:S(2)}, u32[]{:S(2)}) collective-permute-start(f32[3,49152]{1,0:T(4,128)S(1)} %constant_dynamic-update-slice_fusion.refs_1_), channel_id=1, source_target_pairs={{0,4},{4,8},{8,12},{1,5},{5,9},{9,13},{2,6},{6,10},{10,14},{3,7},{... | collective-permute-start | bytes 1769480 | tf_op jit(solution)/shard_map/ppermute | solution.py:465
  21.1 14.5 %copy-start = (f32[16,16384]{1,0:T(8,128)S(1)}, f32[16,16384]{1,0:T(8,128)}, u32[]{:S(2)}) copy-start(f32[16,16384]{1,0:T(8,128)} %shard_map.145.c_ref.refs_4_) | copy-start | bytes 3145732
  21.1 21.3 %copy-start.6 = (f32[3,128]{1,0:T(4,128)S(1)}, f32[3,128]{1,0:T(4,128)}, u32[]{:S(2)}) copy-start(f32[3,128]{1,0:T(4,128)} %param.20) | copy-start | bytes 4612
  35.5 28.7 %copy-start.3 = (f32[3,49152]{1,0:T(4,128)}, f32[3,49152]{1,0:T(4,128)S(1)}, u32[]{:S(2)}) copy-start(f32[3,49152]{1,0:T(4,128)S(1)} %collective-permute-done.1.refs_2_) | copy-start | bytes 1769476
  35.6 28.7 %copy-start.4 = (f32[3,49152]{1,0:T(4,128)}, f32[3,49152]{1,0:T(4,128)S(1)}, u32[]{:S(2)}) copy-start(f32[3,49152]{1,0:T(4,128)S(1)} %collective-permute-done.refs_0_) | copy-start | bytes 1769476
  35.6 46.5 %collective-permute-start.3 = (f32[16,16384]{1,0:T(8,128)S(1)}, f32[16,16384]{1,0:T(8,128)}, u32[]{:S(2)}, u32[]{:S(2)}) collective-permute-start(f32[16,16384]{1,0:T(8,128)S(1)} %copy-done), channel_id=1, source_target_pairs={{4,0},{8,4},{12,8},{5,1},{9,5},{13,9},{6,2},{10,6},{14,10},{7,3},{... | collective-permute-start | bytes 3145736 | tf_op jit(solution)/shard_map/ppermute | solution.py:465
  36.9 45.2 %collective-permute-start.2 = (f32[16,16384]{1,0:T(8,128)S(1)}, f32[16,16384]{1,0:T(8,128)}, u32[]{:S(2)}, u32[]{:S(2)}) collective-permute-start(f32[16,16384]{1,0:T(8,128)S(1)} %copy-done), channel_id=1, source_target_pairs={{0,4},{4,8},{8,12},{1,5},{5,9},{9,13},{2,6},{6,10},{10,14},{3,7},{... | collective-permute-start | bytes 3145736 | tf_op jit(solution)/shard_map/ppermute | solution.py:465
  42.6 21.5 %collective-permute-start.5 = (f32[16,32]{1,0:T(8,128)}, f32[16,32]{1,0:T(8,128)S(1)}, u32[]{:S(2)}, u32[]{:S(2)}) collective-permute-start(f32[16,32]{1,0:T(8,128)} %shard_map.146), channel_id=1, source_target_pairs={{0,12},{12,0},{1,13},{13,1},{2,14},{14,2},{3,15},{15,3},{16,28},{2... | collective-permute-start | bytes 6152 | tf_op jit(solution)/shard_map/ppermute | solution.py:485
  47.3 16.9 %collective-permute-start.4 = (f32[16,32]{1,0:T(8,128)}, f32[16,32]{1,0:T(8,128)S(1)}, u32[]{:S(2)}, u32[]{:S(2)}) collective-permute-start(f32[16,32]{1,0:T(8,128)} %shard_map.146), channel_id=1, source_target_pairs={{0,8},{4,12},{8,0},{12,4},{1,9},{5,13},{9,1},{13,5},{2,10},{6,14},... | collective-permute-start | bytes 6152 | tf_op jit(solution)/shard_map/ppermute | solution.py:485
  65.0 17.1 %copy-start.1 = (f32[16,32768]{1,0:T(8,128)S(1)}, f32[16,32768]{1,0:T(8,128)}, u32[]{:S(2)}) copy-start(f32[16,32768]{1,0:T(8,128)} %refs_4_.1) | copy-start | bytes 6291460
  65.0 24.6 %copy-start.5 = (s32[512,16]{0,1:T(8,128)S(1)}, s32[512,16]{0,1:T(8,128)}, u32[]{:S(2)}) copy-start(s32[512,16]{0,1:T(8,128)} %param.23) | copy-start | bytes 98308
  82.1 55.0 %collective-permute-start.7 = (f32[16,32768]{1,0:T(8,128)S(1)}, f32[16,32768]{1,0:T(8,128)}, u32[]{:S(2)}, u32[]{:S(2)}) collective-permute-start(f32[16,32768]{1,0:T(8,128)S(1)} %copy-done.1), channel_id=1, source_target_pairs={{4,0},{8,4},{12,8},{5,1},{9,5},{13,9},{6,2},{10,6},{14,10},{7,3},{... | collective-permute-start | bytes 6291464 | tf_op jit(solution)/shard_map/ppermute | solution.py:465
  83.4 53.7 %collective-permute-start.6 = (f32[16,32768]{1,0:T(8,128)S(1)}, f32[16,32768]{1,0:T(8,128)}, u32[]{:S(2)}, u32[]{:S(2)}) collective-permute-start(f32[16,32768]{1,0:T(8,128)S(1)} %copy-done.1), channel_id=1, source_target_pairs={{0,4},{4,8},{8,12},{1,5},{5,9},{9,13},{2,6},{6,10},{10,14},{3,7},{... | collective-permute-start | bytes 6291464 | tf_op jit(solution)/shard_map/ppermute | solution.py:465
where the time goes:
time: 199 us; the launch traced here: 197 us
  Pallas kernels  142 us (71%)
  starting transfers between devices  23.3 us (12%)
  waiting for transfers between devices  16.7 us (8%)
  other arithmetic  7.65 us (4%)
  matrix products  3.31 us (2%)
  local copies, waits for them, and re-layouts  2.28 us (1%)
    pallas_call x2, Pallas kernels, pair_sums(): call(body, jax.ShapeDtypeStruct((rows, width), f32), len(args) - 1, scrat...  94.4 us
    pallas_call x1, Pallas kernels, tree_down(): call(body, jax.ShapeDtypeStruct((rows, width), f32), 2, [pltpu.VMEM((2, r...  17.1 us
    ppermute x2, waiting for transfers between devices, local(): parts.append(lax.ppermute(root, 'leaf', rise + fall))  16.7 us
    ppermute x3, starting transfers between devices, local(): lax.ppermute(x, 'leaf', up)  16 us
    pallas_call x1, Pallas kernels, tree_up(): call(body, jax.ShapeDtypeStruct((rows, rank), f32), 2, [pltpu.VMEM((2, ro...  12.1 us
    pallas_call x1, Pallas kernels, leaf_coefs(): call_blocks(body, out, (width, width), (rows, rank), STEPS, 4 * 10 ** 7)  9.92 us
    pallas_call x1, Pallas kernels, leaf_product(): call_blocks(body, out, *sizes, STEPS, 4 * 10 ** 7)  8.89 us
  transfers between devices with their start and end apart: 8, of which 1 were waited for; matrix products, arithmetic and copies ran while one was open for 6% of the time, Pallas kernels for 42%

commit v1 on v0

--- a/solution.py
+++ b/solution.py
@@ -14,7 +14,7 @@
 FEATS = 16
 UNROLL = 64
 WIDE = 2
-STEPS = 8
+STEPS = 4
 VMEM_LIMIT = 58 * 1024 * 1024
 f32, bf16, i32 = jnp.float32, jnp.bfloat16, jnp.int32
 
@@ -125,7 +125,7 @@
             for i, out in zip(ids, outs):
                 o_ref[:, at(i, LANES)] = out
 
-        in_chunks(width // span // STEPS, 8, run)
+        in_chunks(width // span // STEPS, 32, run)
 
     out = jax.ShapeDtypeStruct((rows, width // leaf_pts * rank), f32)
     return call_blocks(body, out, (width, width), (rows, rank), STEPS, 4 * 10**7)(rhs, basis)
@@ -149,7 +149,7 @@
             for i, out in zip(ids, outs):
                 o_ref[:, at(i, span)] = n_ref[:, at(i, span)] + out
 
-        in_chunks(width // span // STEPS, 8, run)
+        in_chunks(width // span // STEPS, 32, run)
 
     out = jax.ShapeDtypeStruct((rows, width), f32)
     far = down.shape[1]
@@ -182,7 +182,7 @@
                 for i, out in zip(ids, outs):
                     dst[:, at(i, out_span)] = out
 
-            in_chunks(here * rank // out_span, 8, run)
+            in_chunks(here * rank // out_span, 32, run)
         last = buf[(levels - 1) % 2, :, : 2 * rank]
         o_ref[...] = last[:, :rank] + last[:, rank:]
 
@@ -223,7 +223,7 @@
                 for i, out in zip(ids, outs):
                     dst[:, at(i, span)] = out
 
-            in_chunks(here * rank // in_span, 8, run)
+            in_chunks(here * rank // in_span, 32, run)
 
     return call(
         body,
@@ -363,7 +363,7 @@
                 for j, out in enumerate(outs):
                     tab[piece * leaves + first * per + j] = out
 
-            in_chunks(width // LANES, 16, fill)
+            in_chunks(width // LANES, 64, fill)
         tab[held] = jnp.zeros(tab.shape[1:], bf16)
         if narrow:
             flat[held] = jnp.zeros(flat.shape[1:], bf16)
@@ -431,7 +431,7 @@
             for c, out in enumerate(outs):
                 o_ref[:, at(start + c, LANES)] = out
 
-        in_chunks(width // LANES, 16, lay)
+        in_chunks(width // LANES, 64, lay)
 
     scratch = [
         pltpu.VMEM((held + 1, FEATS + (0 if narrow else 2 * rows), LANES), bf16),
@@ -475,8 +475,7 @@
     far_list = work_list(far_src - anchor, far_live, WIDE * LANES // rank, 3 * leaves)
 
     root = tree_up(coef, transfer, leaves)
-    halo_coords, coef, root = lax.optimization_barrier((halo_coords, coef, root))
-    coords = [halo_coords[0], coords, halo_coords[1]]
+    halo_coords, root = lax.optimization_barrier((halo_coords, root))
     halo_coef = both_ways(coef)
     parts, origins = [], []
     for s in range(2, size):
@@ -488,6 +487,13 @@
             parts += [lax.ppermute(root, "leaf", rise), lax.ppermute(root, "leaf", fall)]
             origins += [owner - s, owner + s]
 
+    halo_coef, halo_coords, sent = lax.optimization_barrier((halo_coef, halo_coords, rhs))
+    halo_rhs = both_ways(sent)
+    coords = [halo_coords[0], coords, halo_coords[1]]
+    couple = pair_sums(
+        *far_list, coords, width, [halo_coef[0], coef, halo_coef[1]], leaves, rank
+    )
+    parts, couple = lax.optimization_barrier((parts, couple))
     own_proxy = lax.dynamic_slice_in_dim(root_proxies, owner * rank, rank, 1)
     top = jnp.zeros((rows, rank), f32)
     for part, origin in zip(parts, origins):
@@ -498,13 +504,7 @@
         kernel = jnp.where(there, jnp.exp(-dist / spread_sq), 0.0)
         top = top + jnp.einsum("aj,rj->ra", kernel, part, precision=highest)
     down = tree_down(top, transfer, leaves)
-
-    halo_coef, down, sent = lax.optimization_barrier((halo_coef, down, rhs))
-    halo_rhs = both_ways(sent)
-    couple = pair_sums(
-        *far_list, coords, width, [halo_coef[0], coef, halo_coef[1]], leaves, rank
-    )
-    halo_rhs, couple = lax.optimization_barrier((halo_rhs, couple))
+    halo_rhs, down = lax.optimization_barrier((halo_rhs, down))
     near = pair_sums(
         *near_list, coords, 0, [halo_rhs[0], rhs, halo_rhs[1]], leaves, leaf_pts
     )

time: 199 us -> 172 us (0.86)
  the two profiles are of different devices: /device:TPU:4 before, /device:TPU:0 now
where the time goes in v1:
time: 172 us; the launch traced here: 171 us
  Pallas kernels  123 us (72%)
  starting transfers between devices  26.5 us (15%)
  waiting for transfers between devices  9.43 us (5%)
  other arithmetic  5.5 us (3%)
  matrix products  3.33 us (2%)
  local copies, waits for them, and re-layouts  2.29 us (1%)
    pallas_call x2, Pallas kernels, pair_sums(): call(body, jax.ShapeDtypeStruct((rows, width), f32), len(args) - 1, scrat...  85.6 us
    ppermute x3, starting transfers between devices, local(): lax.ppermute(x, 'leaf', up)  18.4 us
    pallas_call x1, Pallas kernels, tree_down(): call(body, jax.ShapeDtypeStruct((rows, width), f32), 2, [pltpu.VMEM((2, r...  13.7 us
    pallas_call x1, Pallas kernels, tree_up(): call(body, jax.ShapeDtypeStruct((rows, rank), f32), 2, [pltpu.VMEM((2, ro...  9.06 us
    ppermute x3, waiting for transfers between devices, local(): lax.ppermute(x, 'leaf', down_pairs)  8.24 us
    pallas_call x1, Pallas kernels, leaf_coefs(): call_blocks(body, out, (width, width), (rows, rank), STEPS, 4 * 10 ** 7)  8.19 us
    pallas_call x1, Pallas kernels, leaf_product(): call_blocks(body, out, *sizes, STEPS, 4 * 10 ** 7)  6.39 us
    ppermute x2, starting transfers between devices, local(): parts.append(lax.ppermute(root, 'leaf', rise + fall))  4.08 us
  transfers between devices with their start and end apart: 8, of which 2 were waited for; matrix products, arithmetic and copies ran while one was open for 5% of the time, Pallas kernels for 43%

profile of v1, /device:TPU:0, one launch (start us, length us, event | category | flops | bytes accessed | tf_op | source)
XLA Modules:
  0.0 170.9 jit_solution(8226257183498074054)
XLA Ops:
  0.0 1.1 constant_dynamic-update-slice_fusion.1
  1.1 1.0 constant_dynamic-update-slice_fusion.refs_1_
  2.2 0.0 copy-start.1
  2.2 0.0 copy-start.5
  2.2 0.0 copy-start.4
  2.2 1.4 collective-permute-start.3
  3.6 6.5 %collective-permute-start.2 = (f32[3,49152]{1,0:T(4,128)S(1)}, f32[3,49152]{1,0:T(4,128)}, u32[]{:S(2)}, u32[]{:S(2)}) collective-permute-start(f32[3,49152]{1,0:T(4,128)S(1)} %constant_dynamic-update-slice_fusion.refs_1_), channel_id=1, source_target_pairs={{0,4},{4,8},{8,12},{1,5},{5,9},{9,13},{2,6},{6,10},{10,14},{3,7},{... | collective-permute-start | bytes 1769480 | tf_op jit(solution)/shard_map/ppermute | solution.py:465
  10.1 8.2 %shard_map.145.c_ref.refs_4_ = f32[16,16384]{1,0:T(8,128)} custom-call(f32[16,32768]{1,0:T(8,128)} %refs_4_.1, f32[32,32768]{1,0:T(8,128)} %b_ref.3), custom_call_target="tpu_custom_call" | custom-call | bytes 40000000 | tf_op jit(solution)/shard_map/pallas_call | solution.py:131
  18.3 0.0 copy-done.1
  18.3 1.3 collective-permute-start.1
  19.6 5.5 %collective-permute-start = (f32[16,16384]{1,0:T(8,128)}, f32[16,16384]{1,0:T(8,128)}, u32[]{:S(2)}, u32[]{:S(2)}) collective-permute-start(f32[16,16384]{1,0:T(8,128)} %shard_map.145.c_ref.refs_4_), channel_id=1, source_target_pairs={{0,4},{4,8},{8,12},{1,5},{5,9},{9,13},{2,6},{6,10},{10,14},{3,7},{... | collective-permute-start | bytes 3145736 | tf_op jit(solution)/shard_map/ppermute | solution.py:465
  25.1 0.0 copy-done.5
  25.2 0.6 fusion.66
  25.8 0.1 select_reduce_fusion.4
  26.0 1.1 select_reduce_fusion.1
  27.1 0.0 copy-done.4
  27.1 0.1 multiply_reduce_fusion
  27.3 1.2 fusion.24
  28.5 0.6 iota_compare_fusion.16
  29.8 0.0 copy-start.2
  29.8 0.0 copy-start
  29.8 0.0 copy-start.3
  29.8 9.1 %shard_map.146 = f32[16,32]{1,0:T(8,128)} custom-call(f32[16,16384]{1,0:T(8,128)} %shard_map.145.c_ref.refs_4_, f32[32,32704]{1,0:T(8,128)} %e_ref.3), custom_call_target="tpu_custom_call" | custom-call | bytes 40000000 | tf_op jit(solution)/shard_map/pallas_call | solution.py:189
  38.9 0.1 convert_reduce_fusion
  39.0 0.0 copy-done.2
  39.0 0.1 select_reduce_fusion.6
  39.1 0.0 collective-permute-done.3.refs_2_
  39.1 0.0 collective-permute-done.2.refs_0_
  39.1 8.2 %collective-permute-done.1.refs_5_ = f32[16,16384]{1,0:T(8,128)} collective-permute-done((f32[16,16384]{1,0:T(8,128)}, f32[16,16384]{1,0:T(8,128)}, u32[]{:S(2)}, u32[]{:S(2)}) %collective-permute-start.1) | collective-permute-done | bytes 1048608 | tf_op jit(solution)/shard_map/ppermute | solution.py:465
  47.4 1.2 collective-permute-done.refs_3_
  48.5 0.0 copy-done
  48.5 1.3 collective-permute-start.5
  49.8 6.4 %collective-permute-start.4 = (f32[16,32768]{1,0:T(8,128)S(1)}, f32[16,32768]{1,0:T(8,128)}, u32[]{:S(2)}, u32[]{:S(2)}) collective-permute-start(f32[16,32768]{1,0:T(8,128)S(1)} %copy-done), channel_id=1, source_target_pairs={{0,4},{4,8},{8,12},{1,5},{5,9},{9,13},{2,6},{6,10},{10,14},{3,7},{... | collective-permute-start | bytes 6291464 | tf_op jit(solution)/shard_map/ppermute | solution.py:465
  56.2 0.2 select_reduce_fusion.5
  56.4 1.1 select_reduce_fusion.3
  57.5 1.2 fusion.18
  58.7 0.0 copy-done.3
  58.8 0.1 constant_dynamic-slice_fusion
  58.8 0.1 multiply_reduce_fusion.2
  58.9 0.6 pad_add_fusion.list_ref
  59.5 4.0 %collective-permute-start.7 = (f32[16,32]{1,0:T(8,128)}, f32[16,32]{1,0:T(8,128)S(1)}, u32[]{:S(2)}, u32[]{:S(2)}) collective-permute-start(f32[16,32]{1,0:T(8,128)} %shard_map.146), channel_id=1, source_target_pairs={{0,12},{12,0},{1,13},{13,1},{2,14},{14,2},{3,15},{15,3},{16,28},{2... | collective-permute-start | bytes 6152 | tf_op jit(solution)/shard_map/ppermute | solution.py:484
  63.6 0.1 collective-permute-start.6
  63.6 0.6 pad_add_fusion.1.list_ref
  64.2 42.0 %shard_map.147.c_ref = f32[16,16384]{1,0:T(8,128)} custom-call(s32[9217]{0:T(1024)} %pad_add_fusion.list_ref, bf16[16,16]{1,0:T(8,128)(2,1)} %constant.148.clone.pick_s_ref, bf16[16,16]{1,0:T(8,128)(2,1)} %constant.149.clone.pick_t_ref, bf16[128,128]{1,0:T(8,128)(2,1)} %constant.150.clone.eye_ref, f32[3,49152]{1,0:T(4,128)} %collective-permute-done.2.refs_0_, ...), custom_call_target="tpu_custom_call" | custom-call | bytes 150000000 | tf_op jit(solution)/shard_map/pallas_call | solution.py:444
  106.2 0.0 collective-permute-done.7
  106.2 0.0 collective-permute-done.6
  106.2 0.1 fusion.36
  106.4 0.8 convolution_add_fusion.r_ref
  107.1 13.7 %shard_map.148.d_ref = f32[16,16384]{1,0:T(8,128)} custom-call(f32[16,32]{1,0:T(8,128)} %convolution_add_fusion.r_ref, f32[32,32704]{1,0:T(8,128)} %e_ref.3), custom_call_target="tpu_custom_call" | custom-call | bytes 40000000 | tf_op jit(solution)/shard_map/pallas_call | solution.py:228
  120.8 0.0 collective-permute-done.5.refs_5_
  120.8 0.0 collective-permute-done.4.refs_3_
  120.8 43.7 %shard_map.149.n_ref = f32[16,32768]{1,0:T(8,128)} custom-call(s32[5121]{0:T(1024)} %pad_add_fusion.1.list_ref, bf16[16,16]{1,0:T(8,128)(2,1)} %constant.148.clone.pick_s_ref, bf16[16,16]{1,0:T(8,128)(2,1)} %constant.149.clone.pick_t_ref, bf16[128,128]{1,0:T(8,128)(2,1)} %constant.150.clone.eye_ref, f32[3,49152]{1,0:T(4,128)} %collective-permute-done.2.refs_0_, ...), custom_call_target="tpu_custom_call" | custom-call | bytes 150000000 | tf_op jit(solution)/shard_map/pallas_call | solution.py:444
  164.5 6.4 %shard_map.150 = f32[16,32768]{1,0:T(8,128)} custom-call(f32[16,16384]{1,0:T(8,128)} %shard_map.148.d_ref, f32[16,16384]{1,0:T(8,128)} %shard_map.147.c_ref, f32[32,32768]{1,0:T(8,128)} %b_ref.3, f32[16,32768]{1,0:T(8,128)} %shard_map.149.n_ref), custom_call_target="tpu_custom_call" | custom-call | bytes 40000000 | tf_op jit(solution)/shard_map/pallas_call | solution.py:157
  (17 shorter events, 0.2 us)
Async XLA Ops:
  2.2 16.2 %copy-start.1 = (f32[3,49152]{1,0:T(4,128)}, f32[3,49152]{1,0:T(4,128)S(1)}, u32[]{:S(2)}) copy-start(f32[3,49152]{1,0:T(4,128)S(1)} %constant_dynamic-update-slice_fusion.refs_1_) | copy-start | bytes 1769476
  2.2 23.0 %copy-start.5 = (s32[512]{0:T(512)S(1)}, s32[512]{0:T(512)}, u32[]{:S(2)}) copy-start(s32[512]{0:T(512)} %param.22) | copy-start | bytes 6148
  2.2 24.9 %copy-start.4 = (s32[512,8]{0,1:T(8,128)S(1)}, s32[512,8]{0,1:T(8,128)}, u32[]{:S(2)}) copy-start(s32[512,8]{0,1:T(8,128)} %param.21) | copy-start | bytes 49156
  2.2 36.9 %collective-permute-start.3 = (f32[3,49152]{1,0:T(4,128)S(1)}, f32[3,49152]{1,0:T(4,128)}, u32[]{:S(2)}, u32[]{:S(2)}) collective-permute-start(f32[3,49152]{1,0:T(4,128)S(1)} %constant_dynamic-update-slice_fusion.refs_1_), channel_id=1, source_target_pairs={{4,0},{8,4},{12,8},{5,1},{9,5},{13,9},{6,2},{10,6},{14,10},{7,3},{... | collective-permute-start | bytes 1769480 | tf_op jit(solution)/shard_map/ppermute | solution.py:465
  3.6 35.5 %collective-permute-start.2 = (f32[3,49152]{1,0:T(4,128)S(1)}, f32[3,49152]{1,0:T(4,128)}, u32[]{:S(2)}, u32[]{:S(2)}) collective-permute-start(f32[3,49152]{1,0:T(4,128)S(1)} %constant_dynamic-update-slice_fusion.refs_1_), channel_id=1, source_target_pairs={{0,4},{4,8},{8,12},{1,5},{5,9},{9,13},{2,6},{6,10},{10,14},{3,7},{... | collective-permute-start | bytes 1769480 | tf_op jit(solution)/shard_map/ppermute | solution.py:465
  18.3 29.0 %collective-permute-start.1 = (f32[16,16384]{1,0:T(8,128)}, f32[16,16384]{1,0:T(8,128)}, u32[]{:S(2)}, u32[]{:S(2)}) collective-permute-start(f32[16,16384]{1,0:T(8,128)} %shard_map.145.c_ref.refs_4_), channel_id=1, source_target_pairs={{4,0},{8,4},{12,8},{5,1},{9,5},{13,9},{6,2},{10,6},{14,10},{7,3},{... | collective-permute-start | bytes 3145736 | tf_op jit(solution)/shard_map/ppermute | solution.py:465
  19.6 28.9 %collective-permute-start = (f32[16,16384]{1,0:T(8,128)}, f32[16,16384]{1,0:T(8,128)}, u32[]{:S(2)}, u32[]{:S(2)}) collective-permute-start(f32[16,16384]{1,0:T(8,128)} %shard_map.145.c_ref.refs_4_), channel_id=1, source_target_pairs={{0,4},{4,8},{8,12},{1,5},{5,9},{9,13},{2,6},{6,10},{10,14},{3,7},{... | collective-permute-start | bytes 3145736 | tf_op jit(solution)/shard_map/ppermute | solution.py:465
  29.8 9.2 %copy-start.2 = (s32[512,16]{0,1:T(8,128)S(1)}, s32[512,16]{0,1:T(8,128)}, u32[]{:S(2)}) copy-start(s32[512,16]{0,1:T(8,128)} %param.23) | copy-start | bytes 98308
  29.8 18.8 %copy-start = (f32[16,32768]{1,0:T(8,128)S(1)}, f32[16,32768]{1,0:T(8,128)}, u32[]{:S(2)}) copy-start(f32[16,32768]{1,0:T(8,128)} %refs_4_.1) | copy-start | bytes 6291460
  29.8 29.0 %copy-start.3 = (f32[3,128]{1,0:T(4,128)S(1)}, f32[3,128]{1,0:T(4,128)}, u32[]{:S(2)}) copy-start(f32[3,128]{1,0:T(4,128)} %param.20) | copy-start | bytes 4612
  48.5 72.3 %collective-permute-start.5 = (f32[16,32768]{1,0:T(8,128)S(1)}, f32[16,32768]{1,0:T(8,128)}, u32[]{:S(2)}, u32[]{:S(2)}) collective-permute-start(f32[16,32768]{1,0:T(8,128)S(1)} %copy-done), channel_id=1, source_target_pairs={{4,0},{8,4},{12,8},{5,1},{9,5},{13,9},{6,2},{10,6},{14,10},{7,3},{... | collective-permute-start | bytes 6291464 | tf_op jit(solution)/shard_map/ppermute | solution.py:465
  49.8 71.0 %collective-permute-start.4 = (f32[16,32768]{1,0:T(8,128)S(1)}, f32[16,32768]{1,0:T(8,128)}, u32[]{:S(2)}, u32[]{:S(2)}) collective-permute-start(f32[16,32768]{1,0:T(8,128)S(1)} %copy-done), channel_id=1, source_target_pairs={{0,4},{4,8},{8,12},{1,5},{5,9},{9,13},{2,6},{6,10},{10,14},{3,7},{... | collective-permute-start | bytes 6291464 | tf_op jit(solution)/shard_map/ppermute | solution.py:465
  59.5 46.7 %collective-permute-start.7 = (f32[16,32]{1,0:T(8,128)}, f32[16,32]{1,0:T(8,128)S(1)}, u32[]{:S(2)}, u32[]{:S(2)}) collective-permute-start(f32[16,32]{1,0:T(8,128)} %shard_map.146), channel_id=1, source_target_pairs={{0,12},{12,0},{1,13},{13,1},{2,14},{14,2},{3,15},{15,3},{16,28},{2... | collective-permute-start | bytes 6152 | tf_op jit(solution)/shard_map/ppermute | solution.py:484
  63.6 42.7 %collective-permute-start.6 = (f32[16,32]{1,0:T(8,128)}, f32[16,32]{1,0:T(8,128)S(1)}, u32[]{:S(2)}, u32[]{:S(2)}) collective-permute-start(f32[16,32]{1,0:T(8,128)} %shard_map.146), channel_id=1, source_target_pairs={{0,8},{4,12},{8,0},{12,4},{1,9},{5,13},{9,1},{13,5},{2,10},{6,14},... | collective-permute-start | bytes 6152 | tf_op jit(solution)/shard_map/ppermute | solution.py:484
